TPU v7x, 128 devices: a whole 4x4x4 slice. The times are simulated.
128 devices in a mesh: group: 8 (over x, core), tp: 16 (over y, z).
Axes of the slice: x: 4, y: 4, z: 4, core: 2. Of those that a mesh axis runs over, the one named last changes fastest.
Arguments:
- prefix_store: bfloat16 [64, 128, 7168], P('group', None, 'tp'), may hold values from -6 to 6
- page_owner: int32 [16, 4], replicated, may hold values from 0 to 63, as said below
- prefix_len: int32 [16], P('group'), may hold values from 1 to 512, 6144 in all
- turn_rows: bfloat16 [16, 256, 7168], P('group', None, 'tp'), may hold values from -6 to 6
- turn_len: int32 [16], P('group'), may hold values from 1 to 256, 3072 in all
- w_query: bfloat16 [7168, 8192], P(None, 'tp'), may hold values from -0.091937622 to 0.091937622
- w_key: bfloat16 [7168, 8192], P(None, 'tp'), may hold values from -0.091937622 to 0.091937622
- w_value: bfloat16 [7168, 8192], P(None, 'tp'), may hold values from -0.0625 to 0.0625
Outputs:
- context: bfloat16 [16, 256, 8192], P('group', None, 'tp')
Inputs may be any that keep to these rules, and one draw needn't show every extreme that they name: `page_owner`: each slot is named once. Slot s is held by index s // 8 of group; conversation c belongs to index c // 2. The pages of one index of group's conversations come from 4 indices of group, exactly 2 pages from each of them.
All inputs are finite; a program needn't handle non-finite values. No bound on the sum of `prefix_len` or of `turn_len` on one device may be relied on, other than what follows from the above.
Results may differ from a plain program's by a relative error of at most 0.011.
Values may be sent and summed in bfloat16 or wider, within the bound.
A program may use at most 128 MiB of HBM per device.

v0:
```python
import jax
import jax.numpy as jnp
from jax import lax
from jax.sharding import PartitionSpec as P

HS = 128


first_head = 48.0
all_heads = 112.0


def add_products(piece, weights):
    return tuple(
        (
            jnp.einsum("pnd,dc->pnc", piece, weight, preferred_element_type=jnp.float32)
            for weight in weights
        )
    )


def body(prefix_store, page_owner, prefix_len, turn_rows, turn_len, w_query, w_key, w_value):
    groups = lax.axis_size("group")
    own_group = lax.axis_index("group")
    slot_count = prefix_store.shape[0]
    page_len = prefix_store.shape[1]
    cap_pages = max(2, slot_count // groups)
    owner = page_owner.reshape(groups, slot_count)
    source = owner // slot_count
    local_slot = owner % slot_count
    order = jnp.arange(slot_count, dtype=jnp.int32)
    earlier = order[None, :] < order[:, None]
    arrival = jnp.sum(
        ((source[:, :, None] == source[:, None, :]) & earlier[None]).astype(jnp.int32), axis=2
    )
    places = jnp.arange(cap_pages, dtype=jnp.int32)
    picked = (source == own_group)[:, :, None] & (arrival[:, :, None] == places[None, None, :])
    send_slot = jnp.sum(jnp.where(picked, local_slot[:, :, None], 0), axis=1)
    own_source = lax.dynamic_index_in_dim(source, own_group, 0, keepdims=False)
    own_arrival = lax.dynamic_index_in_dim(arrival, own_group, 0, keepdims=False)
    receive_slot = own_source * cap_pages + own_arrival
    head_cols = w_key.shape[1]
    conv_count = turn_rows.shape[0]
    turn_span = turn_rows.shape[1]
    chosen = jnp.take(prefix_store, send_slot.reshape(-1), axis=0)
    arrived = lax.all_to_all(
        chosen.reshape((groups, cap_pages) + prefix_store.shape[1:]),
        "group",
        split_axis=0,
        concat_axis=0,
        tiled=True,
    )
    flat = arrived.reshape((groups * cap_pages,) + arrived.shape[2:])
    prefix_source = jnp.take(flat, receive_slot, axis=0)
    prefix_totals = add_products(
        lax.all_gather(prefix_source, "tp", axis=2, tiled=True), (w_key, w_value)
    )
    turn_totals = add_products(
        lax.all_gather(turn_rows, "tp", axis=2, tiled=True), (w_query, w_key, w_value)
    )
    key_prefix = prefix_totals[0].astype(jnp.bfloat16)
    value_prefix = prefix_totals[1].astype(jnp.bfloat16)
    heads_here = head_cols // HS
    prefix_span = slot_count * page_len // conv_count
    key_prefix = key_prefix.reshape(conv_count, prefix_span, heads_here, HS)
    value_prefix = value_prefix.reshape(conv_count, prefix_span, heads_here, HS)
    query = turn_totals[0].astype(jnp.bfloat16).reshape(conv_count, turn_span, heads_here, HS)
    key_turn = turn_totals[1].astype(jnp.bfloat16).reshape(conv_count, turn_span, heads_here, HS)
    value_turn = turn_totals[2].astype(jnp.bfloat16).reshape(conv_count, turn_span, heads_here, HS)
    head_index = (
        lax.axis_index("tp") * heads_here + jnp.arange(heads_here, dtype=jnp.int32)
    ).astype(jnp.float32)
    slopes = 2.0 ** (-8.0 * (first_head + 1.0 + head_index) / all_heads)
    scale = HS ** (-0.5)
    scores_prefix = (
        jnp.einsum("cihd,cphd->chip", query, key_prefix, preferred_element_type=jnp.float32) * scale
    )
    scores_turn = (
        jnp.einsum("cihd,cjhd->chij", query, key_turn, preferred_element_type=jnp.float32) * scale
    )
    rows = jnp.arange(turn_span, dtype=jnp.int32)
    columns = jnp.arange(prefix_span, dtype=jnp.int32)
    distance_prefix = (
        prefix_len[:, None, None] + rows[None, :, None] - columns[None, None, :]
    ).astype(jnp.float32)
    distance_turn = (rows[:, None] - rows[None, :]).astype(jnp.float32)
    scores_prefix = scores_prefix - slopes[None, :, None, None] * distance_prefix[:, None]
    scores_turn = scores_turn - slopes[None, :, None, None] * distance_turn[None, None]
    live_prefix = (columns[None, :] < prefix_len[:, None])[:, None, None, :]
    live_turn = (
        (rows[None, None, :] <= rows[None, :, None])
        & (rows[None, None, :] < turn_len[:, None, None])
    )[:, None]
    scores = jnp.concatenate(
        [
            jnp.where(live_prefix, scores_prefix, -jnp.inf),
            jnp.where(live_turn, scores_turn, -jnp.inf),
        ],
        axis=-1,
    )
    top = jnp.max(scores, axis=-1, keepdims=True)
    expo = jnp.exp(scores - top)
    weights = (expo / jnp.sum(expo, axis=-1, keepdims=True)).astype(jnp.bfloat16)
    values = jnp.concatenate([value_prefix, value_turn], axis=1)
    context = jnp.einsum("chik,ckhd->cihd", weights, values, preferred_element_type=jnp.float32)
    return context.reshape(conv_count, turn_span, head_cols).astype(jnp.bfloat16)


def solution(mesh):
    in_specs = (
        P("group", None, "tp"),
        P(),
        P("group"),
        P("group", None, "tp"),
        P("group"),
        P(None, "tp"),
        P(None, "tp"),
        P(None, "tp"),
    )
    out_specs = P("group", None, "tp")
    return jax.shard_map(body, mesh=mesh, in_specs=in_specs, out_specs=out_specs, check_vma=False)
```

profile of v0, /device:TPU:0, one launch (start us, length us, event | category | flops | bytes accessed | tf_op | source)
XLA Modules:
  0.0 231.9 jit_solution(14033295686325307443)
XLA Ops:
  6.5 0.7 all-gather.5.cloned.1.call-update
  7.3 0.8 copy.27
  8.9 0.9 gather_fusion
  9.8 1.5 broadcast_select_fusion
  11.3 4.4 %all-to-all-start = ((bf16[8,2,128,448]{2,3,1,0:T(8,128)(2,1)}), bf16[8,2,128,448]{2,3,1,0:T(8,128)(2,1)S(1)}, u32[]{:S(2)}, u32[]{:S(2)}) async-start(bf16[8,2,128,448]{2,3,1,0:T(8,128)(2,1)} %broadcast_select_fusion), calls=%async_computation | async-start | bytes 3670016 | tf_op jit(solution)/shard_map/all_to_all | solution.py:46
  15.8 24.3 %all-to-all-done = bf16[8,2,128,448]{2,3,1,0:T(8,128)(2,1)S(1)} async-done(((bf16[8,2,128,448]{2,3,1,0:T(8,128)(2,1)}), bf16[8,2,128,448]{2,3,1,0:T(8,128)(2,1)S(1)}, u32[]{:S(2)}, u32[]{:S(2)}) %all-to-all-start) | async-done | bytes 1835040 | tf_op jit(solution)/shard_map/all_to_all | solution.py:46
  40.1 0.7 gather_fusion.1
  40.8 1.1 broadcast_select_fusion.1
  42.3 1.1 subtract_convert_fusion
  43.4 1.1 broadcast_multiply_fusion
  44.6 33.8 %all-gather.5.cloned.1.call-done = bf16[2,256,7168]{1,2,0:T(8,128)(2,1)} async-done(((bf16[2,256,448]{1,2,0:T(8,128)(2,1)}), bf16[2,256,7168]{1,2,0:T(8,128)(2,1)}) %all-gather.5.cloned.1.call-update) | async-done | bytes 7340048 | tf_op jit(solution)/shard_map/all_gather | solution.py:59
  78.3 9.2 %fusion.25 = bf16[2,256,512]{2,1,0:T(8,128)(2,1)S(1)} fusion(bf16[2,256,7168]{1,2,0:T(8,128)(2,1)} %all-gather.5.cloned.1.call-done, bf16[7168,512]{1,0:T(8,128)(2,1)} %param.15), kind=kOutput, calls=%fused_computation.26 | convolution fusion | flops 3758358528 | bytes 15204352 | tf_op jit(solution)/shard_map/pnd,dc->pnc/dot_general | solution.py:16
  87.7 10.1 %fusion.37 = bf16[2,32,4,8,128]{4,3,2,1,0:T(8,128)(2,1)S(1)} fusion(bf16[2,256,7168]{1,2,0:T(8,128)(2,1)} %all-gather.5.cloned.1.call-done, bf16[7168,512]{1,0:T(8,128)(2,1)} %param.13), kind=kOutput, calls=%fused_computation.30 | convolution fusion | flops 3758358528 | bytes 15204352 | tf_op jit(solution)/shard_map/pnd,dc->pnc/dot_general | solution.py:16
  97.8 9.5 %fusion.34 = bf16[2,32,4,8,128]{4,3,2,1,0:T(8,128)(2,1)S(1)} fusion(bf16[2,256,7168]{1,2,0:T(8,128)(2,1)} %all-gather.5.cloned.1.call-done, bf16[7168,512]{1,0:T(8,128)(2,1)} %param.14), kind=kOutput, calls=%fused_computation.29 | convolution fusion | flops 3758358528 | bytes 15204352 | tf_op jit(solution)/shard_map/pnd,dc->pnc/dot_general | solution.py:16
  107.9 72.8 %all-gather.3.cloned.1.call-done = bf16[8,128,7168]{1,2,0:T(8,128)(2,1)} async-done(((bf16[8,128,448]{1,2,0:T(8,128)(2,1)}), bf16[8,128,7168]{1,2,0:T(8,128)(2,1)}) %all-gather.3.cloned.1.call-update) | async-done | bytes 14680080 | tf_op jit(solution)/shard_map/all_gather | solution.py:56
  180.8 14.0 %fusion.16 = bf16[8,128,512]{2,1,0:T(8,128)(2,1)} fusion(bf16[8,128,7168]{1,2,0:T(8,128)(2,1)} %all-gather.3.cloned.1.call-done, bf16[7168,512]{1,0:T(8,128)(2,1)} %param.15), kind=kOutput, calls=%fused_computation.23 | convolution fusion | flops 7516717056 | bytes 23068672 | tf_op jit(solution)/shard_map/pnd,dc->pnc/dot_general | solution.py:16
  194.7 2.1 reshape.314
  196.9 2.4 %copy.30 = bf16[2,512,4,128]{1,3,2,0:T(8,128)(2,1)} copy(bf16[2,512,4,128]{3,2,1,0:T(4,128)(2,1)} %reshape.314) | data formatting | bytes 2097152 | tf_op jit(solution)/shard_map/reshape | solution.py:66
  199.3 13.9 %fusion.19 = bf16[8,128,512]{2,1,0:T(8,128)(2,1)} fusion(bf16[8,128,7168]{1,2,0:T(8,128)(2,1)} %all-gather.3.cloned.1.call-done, bf16[7168,512]{1,0:T(8,128)(2,1)} %param.14), kind=kOutput, calls=%fused_computation.24 | convolution fusion | flops 7516717056 | bytes 23068672 | tf_op jit(solution)/shard_map/pnd,dc->pnc/dot_general | solution.py:16
  213.2 2.1 reshape.317
  215.3 2.7 %fusion.54 = (f32[2,4,256]{2,1,0:T(4,128)S(1)}, f32[2,4,256,512]{3,2,1,0:T(8,128)S(1)}) fusion(f32[2,256,512]{2,1,0:T(8,128)} %subtract_convert_fusion, f32[4]{0:T(128)S(1)} %multiply_power_fusion, bf16[2,512,4,128]{3,2,1,0:T(4,128)(2,1)} %reshape.317, bf16[2,32,4,8,128]{4,3,2,1,0:T(8,128)(2,1)S(1)} %fusion.37, pred[2,512]{1,0:T(4,128)(4,1)S(1)} %iota_compare_fusion.2), kind=kOutput, calls=%fused_computation.75 | convolution fusion | flops 273676288 | bytes 6824976 | tf_op jit(solution)/shard_map/cihd,cphd->chip/dot_general | solution.py:76
  218.1 1.4 fusion.11
  219.5 3.4 %fusion.22 = bf16[2,4,128,256]{3,2,1,0:T(8,128)(2,1)} fusion(f32[2,4,256,256]{3,2,1,0:T(8,128)S(1)} %get-tuple-element.12, f32[2,4,256,512]{3,2,1,0:T(8,128)S(1)} %get-tuple-element.10, f32[2,4,256]{2,1,0:T(4,128)S(1)} %fusion.11, f32[2,4,256]{2,1,0:T(4,128)S(1)} %reduce_max.22, bf16[2,256,4,128]{1,3,2,0:T(8,128)(2,1)S(1)} %bitcast.66, ...), kind=kOutput, calls=%fused_computation.25 | convolution fusion | flops 412352512 | bytes 8404992 | tf_op jit(solution)/shard_map/chik,ckhd->cihd/dot_general | solution.py:105
  223.0 2.0 copy.37
  (39 shorter events, 2.1 us)
Async XLA Ops:
  6.5 2.3 copy-start
  6.5 71.8 %all-gather.5.cloned.1.call-start = ((), (), s32[]{:S(2)}) async-start(), calls=%async_computation.2 | async-start | bytes 7798784 | tf_op jit(solution)/shard_map/all_gather | solution.py:59
  9.8 32.2 %copy-start.5 = (s32[2]{0:T(128)S(1)}, s32[2]{0:T(128)}, u32[]{:S(2)}) copy-start(s32[2]{0:T(128)} %param.12) | copy-start | bytes 28
  9.8 32.3 %copy-start.4 = (s32[2]{0:T(128)S(1)}, s32[2]{0:T(128)}, u32[]{:S(2)}) copy-start(s32[2]{0:T(128)} %param.10) | copy-start | bytes 28
  11.3 28.8 %all-to-all-start = ((bf16[8,2,128,448]{2,3,1,0:T(8,128)(2,1)}), bf16[8,2,128,448]{2,3,1,0:T(8,128)(2,1)S(1)}, u32[]{:S(2)}, u32[]{:S(2)}) async-start(bf16[8,2,128,448]{2,3,1,0:T(8,128)(2,1)} %broadcast_select_fusion), calls=%async_computation | async-start | bytes 3670016 | tf_op jit(solution)/shard_map/all_to_all | solution.py:46
  15.7 165.1 %all-gather.3.cloned.1.call-start = ((), (), s32[]{:S(2)}) async-start(), calls=%async_computation.1 | async-start | bytes 15597568 | tf_op jit(solution)/shard_map/all_gather | solution.py:56
  97.8 9.5 %copy-start.2 = (f32[4,256,256]{2,1,0:T(8,128)S(1)}, f32[4,256,256]{2,1,0:T(8,128)}, u32[]{:S(2)}) copy-start(f32[4,256,256]{2,1,0:T(8,128)} %broadcast_multiply_fusion) | copy-start | bytes 3145732
  215.3 4.2 %copy-start.3 = (bf16[2,512,4,128]{1,3,2,0:T(8,128)(2,1)S(1)}, bf16[2,512,4,128]{1,3,2,0:T(8,128)(2,1)}, u32[]{:S(2)}) copy-start(bf16[2,512,4,128]{1,3,2,0:T(8,128)(2,1)} %copy.30) | copy-start | bytes 3145732
  219.5 5.5 %copy-start.1 = (bf16[8,128,448]{1,2,0:T(8,128)(2,1)S(1)}, bf16[8,128,448]{1,2,0:T(8,128)(2,1)}, u32[]{:S(2)}) copy-start(bf16[8,128,448]{1,2,0:T(8,128)(2,1)} %param.8) | copy-start | bytes 2752516
Sparse Core Ops, SparseCore 0:
  9.5 68.7 all-gather.4
  80.4 100.2 all-gather.2
where the time goes:
time: 233 us; the launch traced here: 232 us
  waiting for transfers between devices  132 us (57%)
  matrix products  63.5 us (27%)
  between operations  13.6 us (6%)
  local copies, waits for them, and re-layouts  11.7 us (5%)
  other arithmetic  7.08 us (3%)
  starting transfers between devices  4.42 us (2%)
    all_gather x1, waiting for transfers between devices, body(): lax.all_gather(prefix_source, 'tp', axis=2, tiled=True)  72.8 us
    dot_general x5, matrix products, add_products(): jnp.einsum('pnd,dc->pnc', piece, weight, preferred_element_type=jnp.float32)  56.6 us
    all_gather x1, waiting for transfers between devices, body(): lax.all_gather(turn_rows, 'tp', axis=2, tiled=True)  33.8 us
    all_to_all x1, waiting for transfers between devices, body(): lax.all_to_all(chosen.reshape((groups, cap_pages) + prefix_store.shape[1:...  24.3 us
  transfers between devices with their start and end apart: 3, of which 3 were waited for; matrix products, arithmetic and copies ran while one was open for 16% of the time, Pallas kernels for 0%

commit v1 on v0

v1 whole, which is shorter than its diff:
```python
import functools

import jax
import jax.numpy as jnp
from jax import lax
from jax.experimental import pallas as pl
from jax.experimental.pallas import tpu as pltpu
from jax.sharding import PartitionSpec as P

MESH = pl.DeviceIdType.MESH

SIDE = 4
TP = SIDE * SIDE
GROUPS = 8
HS = 128
HEADS_HERE = 4
COLS = HEADS_HERE * HS
WIDTH = 7168
SLICE = WIDTH // TP
PAGE = 128
PAGES = 4
CONVS = 2
TURN = 256
PREFIX = 512
HALF = PAGE // 2
BLOCK = 7 * HALF
PART = BLOCK // 2
TURN_CHUNKS = CONVS * TURN // PAGE
CHUNKS = TURN_CHUNKS + CONVS * PAGES
WIDE = 256
FIRST_HEAD = 48.0
ALL_HEADS = 112.0
BF = jnp.bfloat16
F32 = jnp.float32


def pack(rows, odd):
    wide = rows.astype(F32)
    main = jnp.where(odd, wide[:, 64:], wide[:, : 3 * 128])
    loose = jnp.where(odd, wide[:, :64], wide[:, 3 * 128 :])
    low = jnp.where(odd, loose[HALF:], loose[:HALF])
    high = jnp.where(odd, loose[:HALF], loose[HALF:])
    pieces = [
        main[h * HALF : (h + 1) * HALF, j * 128 : (j + 1) * 128]
        for j in range(3)
        for h in range(2)
    ]
    pieces.append(jnp.concatenate([low, high], axis=1))
    return jnp.concatenate(pieces, axis=0).astype(BF)


def kernel(
    owner_ref,
    prefix_len_ref,
    turn_len_ref,
    store_ref,
    turn_ref,
    wq_ref,
    wk_ref,
    wv_ref,
    out_ref,
    held,
    pages_out,
    pages_in,
    weight,
    whole,
    from_turn,
    from_prefix,
    weight_sem,
    page_send,
    page_recv,
    send_sem,
    recv_sem,
):
    group = lax.axis_index("group")
    tp = lax.axis_index("tp")
    y, z = tp // SIDE, tp % SIDE
    odd = tp % 2 == 1

    neighbour = [
        [((y + 1) % SIDE) * SIDE + z, ((y + SIDE - 1) % SIDE) * SIDE + z],
        [y * SIDE + (z + 1) % SIDE, y * SIDE + (z + SIDE - 1) % SIDE],
    ]

    barrier = pltpu.get_barrier_semaphore()
    for axis in range(2):
        for way in range(2):
            pl.semaphore_signal(
                barrier, inc=1, device_id=(group, neighbour[axis][way]), device_id_type=MESH
            )
    for off in range(1, GROUPS):
        pl.semaphore_signal(
            barrier, inc=1, device_id=((group + off) % GROUPS, tp), device_id_type=MESH
        )

    loads = [
        pltpu.make_async_copy(source, weight.at[:, pl.ds(i * COLS, COLS)], weight_sem.at[i])
        for i, source in enumerate((wq_ref, wk_ref, wv_ref))
    ]
    for load in loads:
        load.start()

    for chunk in range(TURN_CHUNKS):
        rows = turn_ref[chunk // 2, pl.ds((chunk % 2) * PAGE, PAGE), :]
        held[chunk, 0] = pack(rows, odd)

    pl.semaphore_wait(barrier, 4 + GROUPS - 1)

    def copy(chunk, source, target, axis, way, half):
        part = pl.ds(0, BLOCK) if half is None else pl.ds(half * PART, PART)
        sem = 0 if half is None else half
        return pltpu.make_async_remote_copy(
            src_ref=held.at[chunk, source, part],
            dst_ref=held.at[chunk, target, part],
            send_sem=send_sem.at[chunk, target, sem],
            recv_sem=recv_sem.at[chunk, target, sem],
            device_id=(group, neighbour[axis][way]),
            device_id_type=MESH,
        )

    def chunks_of(pair):
        return [(2 * pair, 0), (2 * pair + 1, 1)]

    def near_first(pair):
        return [
            copy(chunk, 0, (3 - 2 * way) * SIDE, axis, way, None)
            for chunk, axis in chunks_of(pair)
            for way in range(2)
        ]

    def far_first(pair):
        return [
            copy(chunk, (3 - 2 * way) * SIDE, 2 * SIDE, axis, way, way)
            for chunk, axis in chunks_of(pair)
            for way in range(2)
        ]

    def near_second(pair, which):
        return [
            copy(chunk, i * SIDE, i * SIDE + 3 - 2 * way, 1 - axis, way, None)
            for i in which
            for chunk, axis in chunks_of(pair)
            for way in range(2)
        ]

    def far_second(pair, which):
        return [
            copy(chunk, i * SIDE + 3 - 2 * way, i * SIDE + 2, 1 - axis, way, way)
            for i in which
            for chunk, axis in chunks_of(pair)
            for way in range(2)
        ]

    def start(copies):
        for one in copies:
            one.start()

    def arrived(copies):
        for one in copies:
            one.wait_recv()

    def left(copies):
        for one in copies:
            one.wait_send()

    def stage_a(pairs):
        for pair in pairs:
            start(near_first(pair))
        for pair in pairs:
            start(near_second(pair, (0,)))

    def stage_b(pairs):
        for pair in pairs:
            arrived(near_first(pair))
            start(far_first(pair))
            start(near_second(pair, (1, 3)))

    def stage_c(pairs):
        for pair in pairs:
            arrived(far_first(pair))
            start(near_second(pair, (2,)))
            arrived(near_second(pair, (0,)))
            start(far_second(pair, (0,)))

    def stage_d(pairs):
        for pair in pairs:
            arrived(near_second(pair, (1, 3)))
            start(far_second(pair, (1, 3)))
        for pair in pairs:
            arrived(near_second(pair, (2,)))
            start(far_second(pair, (2,)))

    def gathered(pair):
        arrived(far_second(pair, (0, 1, 2, 3)))

    def all_left(pair):
        left(near_first(pair))
        left(far_first(pair))
        left(near_second(pair, (0, 1, 2, 3)))

    def owner(page):
        return owner_ref[page // PAGES, page % PAGES]

    def stage_pages(to, carry):
        found = jnp.int32(0)
        first = jnp.int32(0)
        second = jnp.int32(0)
        for j in range(CONVS * PAGES):
            slot = owner(to * (CONVS * PAGES) + j)
            mine = slot // GROUPS == group
            first = jnp.where(mine & (found == 0), slot % GROUPS, first)
            second = jnp.where(mine & (found == 1), slot % GROUPS, second)
            found = found + mine.astype(jnp.int32)
        pages_out[to, 0] = store_ref[first]
        pages_out[to, 1] = store_ref[second]
        return carry

    def exchange(off, at):
        return pltpu.make_async_remote_copy(
            src_ref=pages_out.at[(group + off) % GROUPS],
            dst_ref=pages_in.at[at],
            send_sem=page_send.at[off],
            recv_sem=page_recv.at[off],
            device_id=((group + off) % GROUPS, tp),
            device_id_type=MESH,
        )

    def take_page(i, carry):
        source = owner(group * (CONVS * PAGES) + i) // GROUPS
        earlier = jnp.int32(0)
        for j in range(CONVS * PAGES):
            same = owner(group * (CONVS * PAGES) + j) // GROUPS == source
            earlier = earlier + (same & (j < i)).astype(jnp.int32)
        held[TURN_CHUNKS + i, 0] = pack(pages_in[source, jnp.minimum(earlier, 1)], odd)
        return carry

    lane = lax.broadcasted_iota(jnp.int32, (HALF, 128), 1)

    def lay_out(pair):
        def two(v, carry):
            def slot_of(device, axis):
                on_y = (device // SIDE - y + SIDE) % SIDE
                on_z = (device % SIDE - z + SIDE) % SIDE
                return on_y * SIDE + on_z if axis == 0 else on_z * SIDE + on_y

            base = v * (2 * SLICE)
            for chunk, axis in chunks_of(pair):
                even_at, odd_at = slot_of(2 * v, axis), slot_of(2 * v + 1, axis)

                def piece(slot, i):
                    return held[chunk, slot, pl.ds(i * HALF, HALF), :]

                top = pl.ds(axis * PAGE, HALF)
                low = pl.ds(axis * PAGE + HALF, HALF)
                for j in range(3):
                    for h, rows in enumerate((top, low)):
                        at = pl.multiple_of(base + j * 128, 128)
                        whole[rows, pl.ds(at, 128)] = piece(even_at, 2 * j + h)
                        at = pl.multiple_of(base + (4 + j) * 128, 128)
                        whole[rows, pl.ds(at, 128)] = piece(odd_at, 2 * j + h)
                evens, odds = piece(even_at, 6).astype(F32), piece(odd_at, 6).astype(F32)
                at = pl.multiple_of(base + 3 * 128, 128)
                whole[top, pl.ds(at, 128)] = jnp.where(lane < HALF, evens, odds).astype(BF)
                mixed = pltpu.roll(jnp.where(lane < HALF, odds, evens), HALF, axis=1)
                whole[low, pl.ds(at, 128)] = mixed.astype(BF)
            return carry

        lax.fori_loop(0, TP // 2, two, 0)

    def project(pair):
        lay_out(pair)

        def turn_columns(n, carry):
            at = pl.ds(pl.multiple_of(n * WIDE, WIDE), WIDE)
            term = jnp.dot(whole[...], weight[:, at], preferred_element_type=F32)
            from_turn[pair, :, at] = term.astype(BF)
            return carry

        def prefix_columns(n, carry):
            at = pl.ds(pl.multiple_of(n * WIDE, WIDE), WIDE)
            of = pl.ds(pl.multiple_of(COLS + n * WIDE, WIDE), WIDE)
            term = jnp.dot(whole[...], weight[:, of], preferred_element_type=F32)
            conv, half = (pair - CONVS) // 2, (pair - CONVS) % 2
            from_prefix[conv, pl.ds(half * WIDE, WIDE), at] = term.astype(BF)
            return carry

        if pair < CONVS:
            lax.fori_loop(0, 3 * COLS // WIDE, turn_columns, 0)
        else:
            lax.fori_loop(0, 2 * COLS // WIDE, prefix_columns, 0)

    def attend(conv, head):
        number = (tp * HEADS_HERE + head).astype(F32)
        power = jnp.full((1, 128), 1.0, F32) * (-8.0 * (FIRST_HEAD + 1.0 + number) / ALL_HEADS)
        slope = jnp.exp2(power)[:, :1]

        def columns(which):
            return pl.ds(pl.multiple_of(which * COLS + head * HS, HS), HS)

        def dots(left_side, right_side):
            return lax.dot_general(
                left_side, right_side, (((1,), (1,)), ((), ())), preferred_element_type=F32
            ) * (HS**-0.5)

        query = from_turn[conv, :, columns(0)]
        on_prefix = dots(query, from_prefix[conv, :, columns(0)])
        on_turn = dots(query, from_turn[conv, :, columns(1)])
        prefix_count, turn_count = prefix_len_ref[conv], turn_len_ref[conv]
        i = lax.broadcasted_iota(jnp.int32, (TURN, PREFIX), 0)
        j = lax.broadcasted_iota(jnp.int32, (TURN, PREFIX), 1)
        away = (prefix_count + i - j).astype(F32)
        on_prefix = jnp.where(j < prefix_count, on_prefix - slope * away, -jnp.inf)
        i = lax.broadcasted_iota(jnp.int32, (TURN, TURN), 0)
        j = lax.broadcasted_iota(jnp.int32, (TURN, TURN), 1)
        away = (i - j).astype(F32)
        live = j < jnp.minimum(i + 1, turn_count)
        on_turn = jnp.where(live, on_turn - slope * away, -jnp.inf)
        top = jnp.maximum(
            jnp.max(on_prefix, axis=1, keepdims=True), jnp.max(on_turn, axis=1, keepdims=True)
        )
        on_prefix, on_turn = jnp.exp(on_prefix - top), jnp.exp(on_turn - top)
        share = 1.0 / (
            jnp.sum(on_prefix, axis=1, keepdims=True) + jnp.sum(on_turn, axis=1, keepdims=True)
        )
        context = jnp.dot(
            (on_prefix * share).astype(BF),
            from_prefix[conv, :, columns(1)],
            preferred_element_type=F32,
        ) + jnp.dot(
            (on_turn * share).astype(BF), from_turn[conv, :, columns(2)], preferred_element_type=F32
        )
        out_ref[conv, :, columns(0)] = context.astype(BF)

    def attend_some(conv, lo, hi):
        def one(head, carry):
            attend(conv, head)
            return carry

        lax.fori_loop(lo, hi, one, 0)

    stage_a((0, 1))
    lax.fori_loop(0, GROUPS, stage_pages, 0)
    for off in range(1, GROUPS):
        exchange(off, group).start()
    pages_in[group] = pages_out[group]
    stage_b((0, 1))
    stage_c((0, 1))
    for off in range(1, GROUPS):
        exchange(off, (group - off + GROUPS) % GROUPS).wait()
    lax.fori_loop(0, PAGES, take_page, 0)
    stage_a((2, 3))
    stage_d((0, 1))
    lax.fori_loop(PAGES, 2 * PAGES, take_page, 0)
    stage_b((2, 3))
    for load in loads:
        load.wait()
    gathered(0)
    project(0)
    stage_c((2, 3))
    stage_a((4, 5))
    gathered(1)
    project(1)
    stage_d((2, 3))
    stage_b((4, 5))
    for pair in (0, 1):
        all_left(pair)
        left(far_second(pair, (0, 1, 2, 3)))
    gathered(2)
    project(2)
    stage_c((4, 5))
    gathered(3)
    project(3)
    stage_d((4, 5))
    attend_some(0, 0, HEADS_HERE)
    for pair in (2, 3):
        all_left(pair)
        left(far_second(pair, (0, 1, 2, 3)))
    for pair in (4, 5):
        all_left(pair)
    gathered(4)
    project(4)
    gathered(5)
    project(5)
    for pair in (4, 5):
        left(far_second(pair, (0, 1, 2, 3)))
    attend_some(1, 0, HEADS_HERE)


def body(prefix_store, page_owner, prefix_len, turn_rows, turn_len, w_query, w_key, w_value):
    vmem = pl.BlockSpec(memory_space=pltpu.VMEM)
    smem = pl.BlockSpec(memory_space=pltpu.SMEM)
    hbm = pl.BlockSpec(memory_space=pl.ANY)
    return pl.pallas_call(
        kernel,
        out_shape=jax.ShapeDtypeStruct((CONVS, TURN, COLS), BF),
        in_specs=[smem, smem, smem, vmem, vmem, hbm, hbm, hbm],
        out_specs=vmem,
        scratch_shapes=[
            pltpu.VMEM((CHUNKS, TP, BLOCK, 128), BF),
            pltpu.VMEM((GROUPS, 2, PAGE, SLICE), BF),
            pltpu.VMEM((GROUPS, 2, PAGE, SLICE), BF),
            pltpu.VMEM((WIDTH, 3 * COLS), BF),
            pltpu.VMEM((2 * PAGE, WIDTH), BF),
            pltpu.VMEM((CONVS, TURN, 3 * COLS), BF),
            pltpu.VMEM((CONVS, PREFIX, 2 * COLS), BF),
            pltpu.SemaphoreType.DMA((3,)),
            pltpu.SemaphoreType.DMA((GROUPS,)),
            pltpu.SemaphoreType.DMA((GROUPS,)),
            pltpu.SemaphoreType.DMA((CHUNKS, TP, 2)),
            pltpu.SemaphoreType.DMA((CHUNKS, TP, 2)),
        ],
        compiler_params=pltpu.CompilerParams(
            collective_id=0, has_side_effects=True, vmem_limit_bytes=63 * 2**20
        ),
        cost_estimate=pl.CostEstimate(
            flops=27_000_000_000, bytes_accessed=26_000_000, transcendentals=1_600_000
        ),
        name="resume_attention",
    )(page_owner, prefix_len, turn_len, prefix_store, turn_rows, w_query, w_key, w_value)


def solution(mesh):
    in_specs = (
        P("group", None, "tp"),
        P(),
        P("group"),
        P("group", None, "tp"),
        P("group"),
        P(None, "tp"),
        P(None, "tp"),
        P(None, "tp"),
    )
    out_specs = P("group", None, "tp")
    return jax.shard_map(body, mesh=mesh, in_specs=in_specs, out_specs=out_specs, check_vma=False)
```

time: 233 us -> 150 us (0.64)
  Pallas kernels: 0 us -> 142 us
  waiting for transfers between devices: 132 us -> 0 us
  matrix products: 63.5 us -> 0 us
  between operations: 13.6 us -> 0.01 us
  other arithmetic: 7.08 us -> 0 us
  starting transfers between devices: 4.42 us -> 0 us
  local copies, waits for them, and re-layouts: 11.7 us -> 7.49 us
    pallas_call x0 -> x1, Pallas kernels: none -> 142 us  [body(): pl.pallas_call(kernel, out_shape=jax.ShapeDtypeStruct((CONVS, TURN, COLS)...]
    all_gather x2 -> x0, waiting for transfers between devices: 107 us -> none  [the longest x1 72.8 us: body(): lax.all_gather(prefix_source, 'tp', axis=2, tiled=True)]
    dot_general x8 -> x0, matrix products: 63.5 us -> none  [the longest x5 56.6 us: add_products(): jnp.einsum('pnd,dc->pnc', piece, weight, preferred_element_type=jnp.float32)]
    all_to_all x1 -> x0, waiting for transfers between devices: 24.3 us -> none  [body(): lax.all_to_all(chosen.reshape((groups, cap_pages) + prefix_store.shape[1:...]
    reshape x6 -> x0, local copies, waits for them, and re-layouts: 7.06 us -> none  [the longest x2 4.56 us: body(): value_prefix = value_prefix.reshape(conv_count, prefix_span, heads_here, HS)]
    unnamed x13 -> x4, local copies, waits for them, and re-layouts: 0.79 us -> 7.49 us
    all_to_all x1 -> x0, starting transfers between devices: 4.38 us -> none  [body(): lax.all_to_all(chosen.reshape((groups, cap_pages) + prefix_store.shape[1:...]
    select_n x5 -> x0, other arithmetic: 2.59 us -> none  [the longest x2 1.51 us: body(): chosen = jnp.take(prefix_store, send_slot.reshape(-1), axis=0)]
  transfers between devices with their start and end apart: 3 -> 0, of which waited for: 3 -> 0; matrix products, arithmetic and copies ran while one was open for 16% -> 0% of each run, Pallas kernels for 0% -> 0%
where the time goes in v1:
time: 150 us
  Pallas kernels  142 us (95%)
  local copies, waits for them, and re-layouts  7.49 us (5%)
    pallas_call x1, Pallas kernels, body(): pl.pallas_call(kernel, out_shape=jax.ShapeDtypeStruct((CONVS, TURN, COLS)...  142 us
    unnamed x4, local copies, waits for them, and re-layouts  7.49 us

profile of v1, /device:TPU:0, one launch (start us, length us, event | category | flops | bytes accessed | tf_op | source)
XLA Modules:
  0.0 149.5 jit_solution(848935863380750881)
XLA Ops:
  0.0 1.4 copy.9.owner_ref
  1.4 2.0 %copy.11.turn_ref = bf16[2,256,448]{2,1,0:T(8,128)(2,1)} copy(bf16[2,256,448]{1,2,0:T(8,128)(2,1)} %param.11) | data formatting | bytes 917504 | tf_op args[3]
  3.4 2.3 %copy.10.store_ref = bf16[8,128,448]{2,1,0:T(8,128)(2,1)} copy(bf16[8,128,448]{1,2,0:T(8,128)(2,1)} %param.8) | data formatting | bytes 1835008 | tf_op args[0]
  5.6 142.0 %resume_attention.1 = bf16[2,256,512]{2,1,0:T(8,128)(2,1)} custom-call(s32[16,4]{1,0:T(8,128)} %copy.9.owner_ref, s32[2]{0:T(128)} %prefix_len_ref.1, s32[2]{0:T(128)} %turn_len_ref.1, bf16[8,128,448]{2,1,0:T(8,128)(2,1)} %copy.10.store_ref, bf16[2,256,448]{2,1,0:T(8,128)(2,1)} %copy.11.turn_ref, bf16[7168,512]{1,0:T(8,128)(2,1)} %wq_ref.1, ...), custom_call_target="tpu_custom_call" | custom-call | flops 27000000512 | bytes 26000000 | tf_op jit(solution)/shard_map/resume_attention/pallas_call | solution.py:393
  147.6 1.9 %copy.13 = bf16[2,256,512]{2,1,0:T(8,128)(2,1)} copy(bf16[2,256,512]{2,1,0:T(8,128)(2,1)} %resume_attention.1) | data formatting | bytes 1048576

commit v2 on v1

--- a/solution.py
+++ b/solution.py
@@ -22,9 +22,7 @@
 CONVS = 2
 TURN = 256
 PREFIX = 512
-HALF = PAGE // 2
-BLOCK = 7 * HALF
-PART = BLOCK // 2
+PART = SLICE // 2
 TURN_CHUNKS = CONVS * TURN // PAGE
 CHUNKS = TURN_CHUNKS + CONVS * PAGES
 WIDE = 256
@@ -34,31 +32,21 @@
 F32 = jnp.float32
 
 
-def pack(rows, odd):
-    wide = rows.astype(F32)
-    main = jnp.where(odd, wide[:, 64:], wide[:, : 3 * 128])
-    loose = jnp.where(odd, wide[:, :64], wide[:, 3 * 128 :])
-    low = jnp.where(odd, loose[HALF:], loose[:HALF])
-    high = jnp.where(odd, loose[:HALF], loose[HALF:])
-    pieces = [
-        main[h * HALF : (h + 1) * HALF, j * 128 : (j + 1) * 128]
-        for j in range(3)
-        for h in range(2)
-    ]
-    pieces.append(jnp.concatenate([low, high], axis=1))
-    return jnp.concatenate(pieces, axis=0).astype(BF)
-
-
 def kernel(
     owner_ref,
     prefix_len_ref,
     turn_len_ref,
-    store_ref,
-    turn_ref,
+    store_hbm,
+    turn_hbm,
     wq_ref,
     wk_ref,
     wv_ref,
+    out_hbm,
+    store_ref,
     out_ref,
+    part_top,
+    part_sum,
+    part_context,
     held,
     pages_out,
     pages_in,
@@ -66,6 +54,8 @@
     whole,
     from_turn,
     from_prefix,
+    own_sem,
+    out_sem,
     weight_sem,
     page_send,
     page_recv,
@@ -75,12 +65,24 @@
     group = lax.axis_index("group")
     tp = lax.axis_index("tp")
     y, z = tp // SIDE, tp % SIDE
-    odd = tp % 2 == 1
 
     neighbour = [
         [((y + 1) % SIDE) * SIDE + z, ((y + SIDE - 1) % SIDE) * SIDE + z],
         [y * SIDE + (z + 1) % SIDE, y * SIDE + (z + SIDE - 1) % SIDE],
     ]
+
+    fetch_turn = [
+        pltpu.make_async_copy(
+            turn_hbm.at[chunk // 2, :, pl.ds((chunk % 2) * PAGE, PAGE)],
+            held.at[chunk, 0],
+            own_sem.at[chunk],
+        )
+        for chunk in range(TURN_CHUNKS)
+    ]
+    fetch_store = pltpu.make_async_copy(store_hbm, store_ref, own_sem.at[TURN_CHUNKS])
+    for fetch in fetch_turn:
+        fetch.start()
+    fetch_store.start()
 
     barrier = pltpu.get_barrier_semaphore()
     for axis in range(2):
@@ -97,17 +99,12 @@
         pltpu.make_async_copy(source, weight.at[:, pl.ds(i * COLS, COLS)], weight_sem.at[i])
         for i, source in enumerate((wq_ref, wk_ref, wv_ref))
     ]
-    for load in loads:
-        load.start()
-
-    for chunk in range(TURN_CHUNKS):
-        rows = turn_ref[chunk // 2, pl.ds((chunk % 2) * PAGE, PAGE), :]
-        held[chunk, 0] = pack(rows, odd)
-
+    for fetch in fetch_turn:
+        fetch.wait()
     pl.semaphore_wait(barrier, 4 + GROUPS - 1)
 
     def copy(chunk, source, target, axis, way, half):
-        part = pl.ds(0, BLOCK) if half is None else pl.ds(half * PART, PART)
+        part = pl.ds(0, SLICE) if half is None else pl.ds(half * PART, PART)
         sem = 0 if half is None else half
         return pltpu.make_async_remote_copy(
             src_ref=held.at[chunk, source, part],
@@ -199,7 +196,7 @@
         left(near_second(pair, (0, 1, 2, 3)))
 
     def owner(page):
-        return owner_ref[page // PAGES, page % PAGES]
+        return owner_ref[page % PAGES, page // PAGES]
 
     def stage_pages(to, carry):
         found = jnp.int32(0)
@@ -231,10 +228,8 @@
         for j in range(CONVS * PAGES):
             same = owner(group * (CONVS * PAGES) + j) // GROUPS == source
             earlier = earlier + (same & (j < i)).astype(jnp.int32)
-        held[TURN_CHUNKS + i, 0] = pack(pages_in[source, jnp.minimum(earlier, 1)], odd)
+        held[TURN_CHUNKS + i, 0] = pages_in[source, jnp.minimum(earlier, 1)]
         return carry
-
-    lane = lax.broadcasted_iota(jnp.int32, (HALF, 128), 1)
 
     def lay_out(pair):
         def two(v, carry):
@@ -243,26 +238,10 @@
                 on_z = (device % SIDE - z + SIDE) % SIDE
                 return on_y * SIDE + on_z if axis == 0 else on_z * SIDE + on_y
 
-            base = v * (2 * SLICE)
+            at = pl.ds(pl.multiple_of(v * (2 * SLICE), 128), 2 * SLICE)
             for chunk, axis in chunks_of(pair):
-                even_at, odd_at = slot_of(2 * v, axis), slot_of(2 * v + 1, axis)
-
-                def piece(slot, i):
-                    return held[chunk, slot, pl.ds(i * HALF, HALF), :]
-
-                top = pl.ds(axis * PAGE, HALF)
-                low = pl.ds(axis * PAGE + HALF, HALF)
-                for j in range(3):
-                    for h, rows in enumerate((top, low)):
-                        at = pl.multiple_of(base + j * 128, 128)
-                        whole[rows, pl.ds(at, 128)] = piece(even_at, 2 * j + h)
-                        at = pl.multiple_of(base + (4 + j) * 128, 128)
-                        whole[rows, pl.ds(at, 128)] = piece(odd_at, 2 * j + h)
-                evens, odds = piece(even_at, 6).astype(F32), piece(odd_at, 6).astype(F32)
-                at = pl.multiple_of(base + 3 * 128, 128)
-                whole[top, pl.ds(at, 128)] = jnp.where(lane < HALF, evens, odds).astype(BF)
-                mixed = pltpu.roll(jnp.where(lane < HALF, odds, evens), HALF, axis=1)
-                whole[low, pl.ds(at, 128)] = mixed.astype(BF)
+                blocks = [held[chunk, slot_of(2 * v + k, axis)] for k in range(2)]
+                whole[pl.ds(axis * PAGE, PAGE), at] = jnp.concatenate(blocks, axis=0).T
             return carry
 
         lax.fori_loop(0, TP // 2, two, 0)
@@ -289,59 +268,102 @@
         else:
             lax.fori_loop(0, 2 * COLS // WIDE, prefix_columns, 0)
 
-    def attend(conv, head):
+    def slope_of(head):
         number = (tp * HEADS_HERE + head).astype(F32)
         power = jnp.full((1, 128), 1.0, F32) * (-8.0 * (FIRST_HEAD + 1.0 + number) / ALL_HEADS)
-        slope = jnp.exp2(power)[:, :1]
-
-        def columns(which):
-            return pl.ds(pl.multiple_of(which * COLS + head * HS, HS), HS)
-
-        def dots(left_side, right_side):
-            return lax.dot_general(
-                left_side, right_side, (((1,), (1,)), ((), ())), preferred_element_type=F32
-            ) * (HS**-0.5)
-
-        query = from_turn[conv, :, columns(0)]
-        on_prefix = dots(query, from_prefix[conv, :, columns(0)])
-        on_turn = dots(query, from_turn[conv, :, columns(1)])
-        prefix_count, turn_count = prefix_len_ref[conv], turn_len_ref[conv]
-        i = lax.broadcasted_iota(jnp.int32, (TURN, PREFIX), 0)
-        j = lax.broadcasted_iota(jnp.int32, (TURN, PREFIX), 1)
-        away = (prefix_count + i - j).astype(F32)
-        on_prefix = jnp.where(j < prefix_count, on_prefix - slope * away, -jnp.inf)
+        return jnp.exp2(power)[:, :1]
+
+    def columns(which, head):
+        return pl.ds(pl.multiple_of(which * COLS + head * HS, HS), HS)
+
+    def dots(left_side, right_side):
+        return lax.dot_general(
+            left_side, right_side, (((1,), (1,)), ((), ())), preferred_element_type=F32
+        ) * (HS**-0.5)
+
+    def prefix_scores(conv, head, lo, count):
+        scores = dots(
+            from_turn[conv, :, columns(0, head)], from_prefix[conv, pl.ds(lo, count), columns(0, head)]
+        )
+        i = lax.broadcasted_iota(jnp.int32, (TURN, count), 0)
+        j = lax.broadcasted_iota(jnp.int32, (TURN, count), 1) + lo
+        away = (prefix_len_ref[conv] + i - j).astype(F32)
+        return jnp.where(j < prefix_len_ref[conv], scores - slope_of(head) * away, -jnp.inf)
+
+    def turn_scores(conv, head):
+        scores = dots(from_turn[conv, :, columns(0, head)], from_turn[conv, :, columns(1, head)])
         i = lax.broadcasted_iota(jnp.int32, (TURN, TURN), 0)
         j = lax.broadcasted_iota(jnp.int32, (TURN, TURN), 1)
         away = (i - j).astype(F32)
-        live = j < jnp.minimum(i + 1, turn_count)
-        on_turn = jnp.where(live, on_turn - slope * away, -jnp.inf)
-        top = jnp.maximum(
-            jnp.max(on_prefix, axis=1, keepdims=True), jnp.max(on_turn, axis=1, keepdims=True)
-        )
+        live = j < jnp.minimum(i + 1, turn_len_ref[conv])
+        return jnp.where(live, scores - slope_of(head) * away, -jnp.inf)
+
+    def highest(scores):
+        return jnp.max(scores, axis=1, keepdims=True)
+
+    def summed(scores):
+        return jnp.sum(scores, axis=1, keepdims=True)
+
+    def prefix_values(conv, head, lo, count, weights):
+        return jnp.dot(
+            weights.astype(BF),
+            from_prefix[conv, pl.ds(lo, count), columns(1, head)],
+            preferred_element_type=F32,
+        )
+
+    def turn_values(conv, head, weights):
+        return jnp.dot(
+            weights.astype(BF), from_turn[conv, :, columns(2, head)], preferred_element_type=F32
+        )
+
+    def attend(conv, head):
+        on_prefix, on_turn = prefix_scores(conv, head, 0, PREFIX), turn_scores(conv, head)
+        top = jnp.maximum(highest(on_prefix), highest(on_turn))
         on_prefix, on_turn = jnp.exp(on_prefix - top), jnp.exp(on_turn - top)
-        share = 1.0 / (
-            jnp.sum(on_prefix, axis=1, keepdims=True) + jnp.sum(on_turn, axis=1, keepdims=True)
-        )
-        context = jnp.dot(
-            (on_prefix * share).astype(BF),
-            from_prefix[conv, :, columns(1)],
-            preferred_element_type=F32,
-        ) + jnp.dot(
-            (on_turn * share).astype(BF), from_turn[conv, :, columns(2)], preferred_element_type=F32
-        )
-        out_ref[conv, :, columns(0)] = context.astype(BF)
-
-    def attend_some(conv, lo, hi):
+        share = 1.0 / (summed(on_prefix) + summed(on_turn))
+        context = prefix_values(conv, head, 0, PREFIX, on_prefix * share)
+        context = context + turn_values(conv, head, on_turn * share)
+        out_ref[conv, :, columns(0, head)] = context.astype(BF)
+
+    def attend_early(conv, head):
+        on_prefix, on_turn = prefix_scores(conv, head, 0, PREFIX // 2), turn_scores(conv, head)
+        top = jnp.maximum(highest(on_prefix), highest(on_turn))
+        on_prefix, on_turn = jnp.exp(on_prefix - top), jnp.exp(on_turn - top)
+        part_top[head] = jnp.broadcast_to(top, (TURN, 128))
+        part_sum[head] = jnp.broadcast_to(summed(on_prefix) + summed(on_turn), (TURN, 128))
+        part_context[head] = prefix_values(conv, head, 0, PREFIX // 2, on_prefix) + turn_values(
+            conv, head, on_turn
+        )
+
+    def attend_late(conv, head):
+        on_prefix = prefix_scores(conv, head, PREFIX // 2, PREFIX // 2)
+        early_top = part_top[head, :, :1]
+        top = jnp.maximum(early_top, highest(on_prefix))
+        on_prefix = jnp.exp(on_prefix - top)
+        kept = jnp.exp(early_top - top)
+        total = part_sum[head, :, :1] * kept + summed(on_prefix)
+        context = part_context[head] * kept + prefix_values(
+            conv, head, PREFIX // 2, PREFIX // 2, on_prefix
+        )
+        out_ref[conv, :, columns(0, head)] = (context * (1.0 / total)).astype(BF)
+
+    def some_heads(attention, conv, lo, hi):
         def one(head, carry):
-            attend(conv, head)
+            attention(conv, head)
             return carry
 
         lax.fori_loop(lo, hi, one, 0)
 
+    def give(conv):
+        return pltpu.make_async_copy(out_ref.at[conv], out_hbm.at[conv], out_sem.at[conv])
+
     stage_a((0, 1))
+    fetch_store.wait()
     lax.fori_loop(0, GROUPS, stage_pages, 0)
     for off in range(1, GROUPS):
         exchange(off, group).start()
+    for load in loads:
+        load.start()
     pages_in[group] = pages_out[group]
     stage_b((0, 1))
     stage_c((0, 1))
@@ -357,52 +379,66 @@
     gathered(0)
     project(0)
     stage_c((2, 3))
-    stage_a((4, 5))
+    stage_a((4,))
     gathered(1)
     project(1)
     stage_d((2, 3))
-    stage_b((4, 5))
+    stage_b((4,))
     for pair in (0, 1):
         all_left(pair)
         left(far_second(pair, (0, 1, 2, 3)))
     gathered(2)
     project(2)
-    stage_c((4, 5))
+    stage_c((4,))
+    stage_a((5,))
     gathered(3)
     project(3)
-    stage_d((4, 5))
-    attend_some(0, 0, HEADS_HERE)
-    for pair in (2, 3):
+    stage_d((4,))
+    stage_b((5,))
+    some_heads(attend, 0, 0, 2)
+    stage_c((5,))
+    gathered(4)
+    project(4)
+    stage_d((5,))
+    some_heads(attend, 0, 2, HEADS_HERE)
+    give(0).start()
+    some_heads(attend_early, 1, 0, HEADS_HERE)
+    for pair in (2, 3, 4):
         all_left(pair)
         left(far_second(pair, (0, 1, 2, 3)))
-    for pair in (4, 5):
-        all_left(pair)
-    gathered(4)
-    project(4)
+    all_left(5)
     gathered(5)
     project(5)
-    for pair in (4, 5):
-        left(far_second(pair, (0, 1, 2, 3)))
-    attend_some(1, 0, HEADS_HERE)
+    some_heads(attend_late, 1, 0, HEADS_HERE)
+    give(1).start()
+    left(far_second(5, (0, 1, 2, 3)))
+    give(0).wait()
+    give(1).wait()
 
 
 def body(prefix_store, page_owner, prefix_len, turn_rows, turn_len, w_query, w_key, w_value):
-    vmem = pl.BlockSpec(memory_space=pltpu.VMEM)
     smem = pl.BlockSpec(memory_space=pltpu.SMEM)
     hbm = pl.BlockSpec(memory_space=pl.ANY)
     return pl.pallas_call(
         kernel,
         out_shape=jax.ShapeDtypeStruct((CONVS, TURN, COLS), BF),
-        in_specs=[smem, smem, smem, vmem, vmem, hbm, hbm, hbm],
-        out_specs=vmem,
+        in_specs=[smem, smem, smem, hbm, hbm, hbm, hbm, hbm],
+        out_specs=hbm,
         scratch_shapes=[
-            pltpu.VMEM((CHUNKS, TP, BLOCK, 128), BF),
-            pltpu.VMEM((GROUPS, 2, PAGE, SLICE), BF),
-            pltpu.VMEM((GROUPS, 2, PAGE, SLICE), BF),
+            pltpu.VMEM((GROUPS, SLICE, PAGE), BF),
+            pltpu.VMEM((CONVS, TURN, COLS), BF),
+            pltpu.VMEM((HEADS_HERE, TURN, 128), F32),
+            pltpu.VMEM((HEADS_HERE, TURN, 128), F32),
+            pltpu.VMEM((HEADS_HERE, TURN, HS), F32),
+            pltpu.VMEM((CHUNKS, TP, SLICE, 128), BF),
+            pltpu.VMEM((GROUPS, 2, SLICE, PAGE), BF),
+            pltpu.VMEM((GROUPS, 2, SLICE, PAGE), BF),
             pltpu.VMEM((WIDTH, 3 * COLS), BF),
             pltpu.VMEM((2 * PAGE, WIDTH), BF),
             pltpu.VMEM((CONVS, TURN, 3 * COLS), BF),
             pltpu.VMEM((CONVS, PREFIX, 2 * COLS), BF),
+            pltpu.SemaphoreType.DMA((TURN_CHUNKS + 1,)),
+            pltpu.SemaphoreType.DMA((CONVS,)),
             pltpu.SemaphoreType.DMA((3,)),
             pltpu.SemaphoreType.DMA((GROUPS,)),
             pltpu.SemaphoreType.DMA((GROUPS,)),
@@ -416,7 +452,16 @@
             flops=27_000_000_000, bytes_accessed=26_000_000, transcendentals=1_600_000
         ),
         name="resume_attention",
-    )(page_owner, prefix_len, turn_len, prefix_store, turn_rows, w_query, w_key, w_value)
+    )(
+        page_owner.T,
+        prefix_len,
+        turn_len,
+        jnp.swapaxes(prefix_store, 1, 2),
+        jnp.swapaxes(turn_rows, 1, 2),
+        w_query,
+        w_key,
+        w_value,
+    )
 
 
 def solution(mesh):

time: 150 us -> 140 us (0.933)
  local copies, waits for them, and re-layouts: 7.49 us -> 1.87 us
  Pallas kernels: 142 us -> 138 us
    unnamed x4 -> x1, local copies, waits for them, and re-layouts: 7.49 us -> 1.87 us
    pallas_call x1, Pallas kernels: 142 us -> 138 us  [body(): pl.pallas_call(kernel, out_shape=jax.ShapeDtypeStruct((CONVS, TURN, COLS)...]
where the time goes in v2:
time: 140 us
  Pallas kernels  138 us (99%)
  local copies, waits for them, and re-layouts  1.87 us (1%)
    pallas_call x1, Pallas kernels, body(): pl.pallas_call(kernel, out_shape=jax.ShapeDtypeStruct((CONVS, TURN, COLS)...  138 us

profile of v2, /device:TPU:0, one launch (start us, length us, event | category | flops | bytes accessed | tf_op | source)
XLA Modules:
  0.0 140.1 jit_solution(9355229077587802401)
XLA Ops:
  0.0 138.2 %resume_attention.1 = bf16[2,256,512]{2,1,0:T(8,128)(2,1)} custom-call(s32[4,16]{1,0:T(4,128)} %bitcast.5, s32[2]{0:T(128)} %prefix_len_ref.1, s32[2]{0:T(128)} %turn_len_ref.1, bf16[8,448,128]{2,1,0:T(8,128)(2,1)} %bitcast.3, bf16[2,448,256]{2,1,0:T(8,128)(2,1)} %bitcast.4, bf16[7168,512]{1,0:T(8,128)(2,1)} %wq_ref.1, bf16[7168,512]{1,0:T(8,128)(2,1)} %wk_ref.1, ...), custom_call_target="tpu_custom_call" | custom-call | flops 27000000512 | bytes 26000000 | tf_op jit(solution)/shard_map/resume_attention/pallas_call | solution.py:422
  138.2 1.9 %copy.10 = bf16[2,256,512]{2,1,0:T(8,128)(2,1)} copy(bf16[2,256,512]{2,1,0:T(8,128)(2,1)} %resume_attention.1) | data formatting | bytes 1048576

commit v3 on v2

--- a/solution.py
+++ b/solution.py
@@ -23,6 +23,7 @@
 TURN = 256
 PREFIX = 512
 PART = SLICE // 2
+SENT = 15
 TURN_CHUNKS = CONVS * TURN // PAGE
 CHUNKS = TURN_CHUNKS + CONVS * PAGES
 WIDE = 256
@@ -109,7 +110,7 @@
         return pltpu.make_async_remote_copy(
             src_ref=held.at[chunk, source, part],
             dst_ref=held.at[chunk, target, part],
-            send_sem=send_sem.at[chunk, target, sem],
+            send_sem=send_sem.at[chunk],
             recv_sem=recv_sem.at[chunk, target, sem],
             device_id=(group, neighbour[axis][way]),
             device_id_type=MESH,
@@ -156,10 +157,6 @@
         for one in copies:
             one.wait_recv()
 
-    def left(copies):
-        for one in copies:
-            one.wait_send()
-
     def stage_a(pairs):
         for pair in pairs:
             start(near_first(pair))
@@ -191,9 +188,16 @@
         arrived(far_second(pair, (0, 1, 2, 3)))
 
     def all_left(pair):
-        left(near_first(pair))
-        left(far_first(pair))
-        left(near_second(pair, (0, 1, 2, 3)))
+        for chunk, axis in chunks_of(pair):
+            blocks = held.at[chunk, pl.ds(0, SENT)]
+            pltpu.make_async_remote_copy(
+                src_ref=blocks,
+                dst_ref=blocks,
+                send_sem=send_sem.at[chunk],
+                recv_sem=recv_sem.at[chunk, 0, 0],
+                device_id=(group, neighbour[axis][0]),
+                device_id_type=MESH,
+            ).wait_send()
 
     def owner(page):
         return owner_ref[page % PAGES, page // PAGES]
@@ -268,12 +272,19 @@
         else:
             lax.fori_loop(0, 2 * COLS // WIDE, prefix_columns, 0)
 
+    def last_columns(n):
+        of = pl.ds(COLS + n * WIDE, WIDE)
+        term = jnp.dot(whole[...], weight[:, of], preferred_element_type=F32)
+        from_prefix[CONVS - 1, pl.ds(WIDE, WIDE), pl.ds(n * WIDE, WIDE)] = term.astype(BF)
+
     def slope_of(head):
-        number = (tp * HEADS_HERE + head).astype(F32)
+        number = jnp.asarray(tp * HEADS_HERE + head, F32)
         power = jnp.full((1, 128), 1.0, F32) * (-8.0 * (FIRST_HEAD + 1.0 + number) / ALL_HEADS)
         return jnp.exp2(power)[:, :1]
 
     def columns(which, head):
+        if isinstance(head, int):
+            return pl.ds(which * COLS + head * HS, HS)
         return pl.ds(pl.multiple_of(which * COLS + head * HS, HS), HS)
 
     def dots(left_side, right_side):
@@ -384,9 +395,6 @@
     project(1)
     stage_d((2, 3))
     stage_b((4,))
-    for pair in (0, 1):
-        all_left(pair)
-        left(far_second(pair, (0, 1, 2, 3)))
     gathered(2)
     project(2)
     stage_c((4,))
@@ -403,15 +411,19 @@
     some_heads(attend, 0, 2, HEADS_HERE)
     give(0).start()
     some_heads(attend_early, 1, 0, HEADS_HERE)
-    for pair in (2, 3, 4):
+    gathered(5)
+    lay_out(5)
+    last_columns(0)
+    last_columns(2)
+    attend_late(1, 0)
+    last_columns(1)
+    attend_late(1, 1)
+    last_columns(3)
+    attend_late(1, 2)
+    attend_late(1, 3)
+    give(1).start()
+    for pair in range(CHUNKS // 2):
         all_left(pair)
-        left(far_second(pair, (0, 1, 2, 3)))
-    all_left(5)
-    gathered(5)
-    project(5)
-    some_heads(attend_late, 1, 0, HEADS_HERE)
-    give(1).start()
-    left(far_second(5, (0, 1, 2, 3)))
     give(0).wait()
     give(1).wait()
 
@@ -442,7 +454,7 @@
             pltpu.SemaphoreType.DMA((3,)),
             pltpu.SemaphoreType.DMA((GROUPS,)),
             pltpu.SemaphoreType.DMA((GROUPS,)),
-            pltpu.SemaphoreType.DMA((CHUNKS, TP, 2)),
+            pltpu.SemaphoreType.DMA((CHUNKS,)),
             pltpu.SemaphoreType.DMA((CHUNKS, TP, 2)),
         ],
         compiler_params=pltpu.CompilerParams(

time: 140 us -> 136 us (0.971)
  Pallas kernels: 138 us -> 133 us
    pallas_call x1, Pallas kernels: 138 us -> 133 us  [body(): pl.pallas_call(kernel, out_shape=jax.ShapeDtypeStruct((CONVS, TURN, COLS)...]
where the time goes in v3:
time: 136 us; the launch traced here: 135 us
  Pallas kernels  133 us (98%)
  local copies, waits for them, and re-layouts  1.87 us (1%)
    pallas_call x1, Pallas kernels, body(): pl.pallas_call(kernel, out_shape=jax.ShapeDtypeStruct((CONVS, TURN, COLS)...  133 us

profile of v3, /device:TPU:0, one launch (start us, length us, event | category | flops | bytes accessed | tf_op | source)
XLA Modules:
  0.0 135.4 jit_solution(13515462280367394425)
XLA Ops:
  0.0 133.5 %resume_attention.1 = bf16[2,256,512]{2,1,0:T(8,128)(2,1)} custom-call(s32[4,16]{1,0:T(4,128)} %bitcast.5, s32[2]{0:T(128)} %prefix_len_ref.1, s32[2]{0:T(128)} %turn_len_ref.1, bf16[8,448,128]{2,1,0:T(8,128)(2,1)} %bitcast.3, bf16[2,448,256]{2,1,0:T(8,128)(2,1)} %bitcast.4, bf16[7168,512]{1,0:T(8,128)(2,1)} %wq_ref.1, bf16[7168,512]{1,0:T(8,128)(2,1)} %wk_ref.1, ...), custom_call_target="tpu_custom_call" | custom-call | flops 27000000512 | bytes 26000000 | tf_op jit(solution)/shard_map/resume_attention/pallas_call | solution.py:434
  133.5 1.9 %copy.10 = bf16[2,256,512]{2,1,0:T(8,128)(2,1)} copy(bf16[2,256,512]{2,1,0:T(8,128)(2,1)} %resume_attention.1) | data formatting | bytes 1048576

commit v4 on v3

--- a/solution.py
+++ b/solution.py
@@ -104,14 +104,13 @@
         fetch.wait()
     pl.semaphore_wait(barrier, 4 + GROUPS - 1)
 
-    def copy(chunk, source, target, axis, way, half):
+    def copy(chunk, source, target, axis, way, half, stage):
         part = pl.ds(0, SLICE) if half is None else pl.ds(half * PART, PART)
-        sem = 0 if half is None else half
         return pltpu.make_async_remote_copy(
             src_ref=held.at[chunk, source, part],
             dst_ref=held.at[chunk, target, part],
             send_sem=send_sem.at[chunk],
-            recv_sem=recv_sem.at[chunk, target, sem],
+            recv_sem=recv_sem.at[chunk, stage],
             device_id=(group, neighbour[axis][way]),
             device_id_type=MESH,
         )
@@ -121,21 +120,21 @@
 
     def near_first(pair):
         return [
-            copy(chunk, 0, (3 - 2 * way) * SIDE, axis, way, None)
+            copy(chunk, 0, (3 - 2 * way) * SIDE, axis, way, None, 0)
             for chunk, axis in chunks_of(pair)
             for way in range(2)
         ]
 
     def far_first(pair):
         return [
-            copy(chunk, (3 - 2 * way) * SIDE, 2 * SIDE, axis, way, way)
+            copy(chunk, (3 - 2 * way) * SIDE, 2 * SIDE, axis, way, way, 1)
             for chunk, axis in chunks_of(pair)
             for way in range(2)
         ]
 
     def near_second(pair, which):
         return [
-            copy(chunk, i * SIDE, i * SIDE + 3 - 2 * way, 1 - axis, way, None)
+            copy(chunk, i * SIDE, i * SIDE + 3 - 2 * way, 1 - axis, way, None, (2, 3, 4, 3)[i])
             for i in which
             for chunk, axis in chunks_of(pair)
             for way in range(2)
@@ -143,7 +142,7 @@
 
     def far_second(pair, which):
         return [
-            copy(chunk, i * SIDE + 3 - 2 * way, i * SIDE + 2, 1 - axis, way, way)
+            copy(chunk, i * SIDE + 3 - 2 * way, i * SIDE + 2, 1 - axis, way, way, 5)
             for i in which
             for chunk, axis in chunks_of(pair)
             for way in range(2)
@@ -153,9 +152,17 @@
         for one in copies:
             one.start()
 
-    def arrived(copies):
-        for one in copies:
-            one.wait_recv()
+    def arrived(pair, stage, count):
+        for chunk, axis in chunks_of(pair):
+            blocks = held.at[chunk, pl.ds(0, count)]
+            pltpu.make_async_remote_copy(
+                src_ref=blocks,
+                dst_ref=blocks,
+                send_sem=send_sem.at[chunk],
+                recv_sem=recv_sem.at[chunk, stage],
+                device_id=(group, neighbour[axis][0]),
+                device_id_type=MESH,
+            ).wait_recv()
 
     def stage_a(pairs):
         for pair in pairs:
@@ -165,27 +172,27 @@
 
     def stage_b(pairs):
         for pair in pairs:
-            arrived(near_first(pair))
+            arrived(pair, 0, 2)
             start(far_first(pair))
             start(near_second(pair, (1, 3)))
 
     def stage_c(pairs):
         for pair in pairs:
-            arrived(far_first(pair))
+            arrived(pair, 1, 1)
             start(near_second(pair, (2,)))
-            arrived(near_second(pair, (0,)))
+            arrived(pair, 2, 2)
             start(far_second(pair, (0,)))
 
     def stage_d(pairs):
         for pair in pairs:
-            arrived(near_second(pair, (1, 3)))
+            arrived(pair, 3, 4)
             start(far_second(pair, (1, 3)))
         for pair in pairs:
-            arrived(near_second(pair, (2,)))
+            arrived(pair, 4, 2)
             start(far_second(pair, (2,)))
 
     def gathered(pair):
-        arrived(far_second(pair, (0, 1, 2, 3)))
+        arrived(pair, 5, 4)
 
     def all_left(pair):
         for chunk, axis in chunks_of(pair):
@@ -194,7 +201,7 @@
                 src_ref=blocks,
                 dst_ref=blocks,
                 send_sem=send_sem.at[chunk],
-                recv_sem=recv_sem.at[chunk, 0, 0],
+                recv_sem=recv_sem.at[chunk, 0],
                 device_id=(group, neighbour[axis][0]),
                 device_id_type=MESH,
             ).wait_send()
@@ -455,7 +462,7 @@
             pltpu.SemaphoreType.DMA((GROUPS,)),
             pltpu.SemaphoreType.DMA((GROUPS,)),
             pltpu.SemaphoreType.DMA((CHUNKS,)),
-            pltpu.SemaphoreType.DMA((CHUNKS, TP, 2)),
+            pltpu.SemaphoreType.DMA((CHUNKS, 6)),
         ],
         compiler_params=pltpu.CompilerParams(
             collective_id=0, has_side_effects=True, vmem_limit_bytes=63 * 2**20

time: 136 us -> 133 us (0.978)
  Pallas kernels: 133 us -> 131 us
    pallas_call x1, Pallas kernels: 133 us -> 131 us  [body(): pl.pallas_call(kernel, out_shape=jax.ShapeDtypeStruct((CONVS, TURN, COLS)...]
where the time goes in v4:
time: 133 us
  Pallas kernels  131 us (98%)
  local copies, waits for them, and re-layouts  1.87 us (1%)
    pallas_call x1, Pallas kernels, body(): pl.pallas_call(kernel, out_shape=jax.ShapeDtypeStruct((CONVS, TURN, COLS)...  131 us

profile of v4, /device:TPU:0, one launch (start us, length us, event | category | flops | bytes accessed | tf_op | source)
XLA Modules:
  0.0 132.5 jit_solution(14330884104719336433)
XLA Ops:
  0.0 130.7 %resume_attention.1 = bf16[2,256,512]{2,1,0:T(8,128)(2,1)} custom-call(s32[4,16]{1,0:T(4,128)} %bitcast.5, s32[2]{0:T(128)} %prefix_len_ref.1, s32[2]{0:T(128)} %turn_len_ref.1, bf16[8,448,128]{2,1,0:T(8,128)(2,1)} %bitcast.3, bf16[2,448,256]{2,1,0:T(8,128)(2,1)} %bitcast.4, bf16[7168,512]{1,0:T(8,128)(2,1)} %wq_ref.1, bf16[7168,512]{1,0:T(8,128)(2,1)} %wk_ref.1, ...), custom_call_target="tpu_custom_call" | custom-call | flops 27000000512 | bytes 26000000 | tf_op jit(solution)/shard_map/resume_attention/pallas_call | solution.py:441
  130.7 1.9 %copy.10 = bf16[2,256,512]{2,1,0:T(8,128)(2,1)} copy(bf16[2,256,512]{2,1,0:T(8,128)(2,1)} %resume_attention.1) | data formatting | bytes 1048576

commit v5 on v4

--- a/solution.py
+++ b/solution.py
@@ -242,17 +242,36 @@
         held[TURN_CHUNKS + i, 0] = pages_in[source, jnp.minimum(earlier, 1)]
         return carry
 
+    def lay_two(chunk, axis, v):
+        def slot_of(device):
+            on_y = (device // SIDE - y + SIDE) % SIDE
+            on_z = (device % SIDE - z + SIDE) % SIDE
+            return on_y * SIDE + on_z if axis == 0 else on_z * SIDE + on_y
+
+        at = pl.ds(pl.multiple_of(v * (2 * SLICE), 128), 2 * SLICE)
+        blocks = [held[chunk, slot_of(2 * v + k)] for k in range(2)]
+        whole[pl.ds(axis * PAGE, PAGE), at] = jnp.concatenate(blocks, axis=0).T
+
+    def lay_early(pair):
+        for chunk, axis in chunks_of(pair):
+            for n in range(4 if axis == 0 else 6):
+                if axis == 0:
+                    lay_two(chunk, axis, 2 * n + 1 - (z + 2) % SIDE // 2)
+                else:
+                    lay_two(chunk, axis, 2 * ((y + 3 + n // 2) % SIDE) + n % 2)
+
+    def lay_late(pair):
+        for chunk, axis in chunks_of(pair):
+            for n in range(4 if axis == 0 else 2):
+                if axis == 0:
+                    lay_two(chunk, axis, 2 * n + (z + 2) % SIDE // 2)
+                else:
+                    lay_two(chunk, axis, 2 * ((y + 2) % SIDE) + n)
+
     def lay_out(pair):
         def two(v, carry):
-            def slot_of(device, axis):
-                on_y = (device // SIDE - y + SIDE) % SIDE
-                on_z = (device % SIDE - z + SIDE) % SIDE
-                return on_y * SIDE + on_z if axis == 0 else on_z * SIDE + on_y
-
-            at = pl.ds(pl.multiple_of(v * (2 * SLICE), 128), 2 * SLICE)
             for chunk, axis in chunks_of(pair):
-                blocks = [held[chunk, slot_of(2 * v + k, axis)] for k in range(2)]
-                whole[pl.ds(axis * PAGE, PAGE), at] = jnp.concatenate(blocks, axis=0).T
+                lay_two(chunk, axis, v)
             return carry
 
         lax.fori_loop(0, TP // 2, two, 0)
@@ -418,8 +437,9 @@
     some_heads(attend, 0, 2, HEADS_HERE)
     give(0).start()
     some_heads(attend_early, 1, 0, HEADS_HERE)
+    lay_early(5)
     gathered(5)
-    lay_out(5)
+    lay_late(5)
     last_columns(0)
     last_columns(2)
     attend_late(1, 0)

time: 133 us -> 132 us (level)
  no operation moved by 1% of the time
where the time goes in v5:
time: 132 us
  Pallas kernels  130 us (98%)
  local copies, waits for them, and re-layouts  1.87 us (1%)
    pallas_call x1, Pallas kernels, body(): pl.pallas_call(kernel, out_shape=jax.ShapeDtypeStruct((CONVS, TURN, COLS)...  130 us

profile of v5, /device:TPU:0, one launch (start us, length us, event | category | flops | bytes accessed | tf_op | source)
XLA Modules:
  0.0 132.1 jit_solution(7212569238536632877)
XLA Ops:
  0.0 130.2 %resume_attention.1 = bf16[2,256,512]{2,1,0:T(8,128)(2,1)} custom-call(s32[4,16]{1,0:T(4,128)} %bitcast.5, s32[2]{0:T(128)} %prefix_len_ref.1, s32[2]{0:T(128)} %turn_len_ref.1, bf16[8,448,128]{2,1,0:T(8,128)(2,1)} %bitcast.3, bf16[2,448,256]{2,1,0:T(8,128)(2,1)} %bitcast.4, bf16[7168,512]{1,0:T(8,128)(2,1)} %wq_ref.1, bf16[7168,512]{1,0:T(8,128)(2,1)} %wk_ref.1, ...), custom_call_target="tpu_custom_call" | custom-call | flops 27000000512 | bytes 26000000 | tf_op jit(solution)/shard_map/resume_attention/pallas_call | solution.py:461
  130.2 1.9 %copy.10 = bf16[2,256,512]{2,1,0:T(8,128)(2,1)} copy(bf16[2,256,512]{2,1,0:T(8,128)(2,1)} %resume_attention.1) | data formatting | bytes 1048576
